TPU v7x, 128 devices: a whole 4x4x4 slice. The times are simulated.
128 devices in a mesh: row: 8 (over z_lo, y), col: 4 (over x), ch: 4 (over z_hi, core).
Axes of the slice: x: 4, y: 4, z: 4 (z_hi: 2, z_lo: 2; z = z_hi * 2 + z_lo), core: 2. Of those that a mesh axis runs over, the one named last changes fastest.
Arguments:
- pair: bfloat16 [960, 960, 128], P(('row', 'ch'), 'col'), may hold values from -400 to 400
- norm_gain: float32 [128], replicated, may hold values from 0.25 to 1.75
- norm_shift: float32 [128], replicated, may hold values from -3 to 3
- proj_weight: bfloat16 [128, 4, 128], replicated, may hold values from -0.5 to 0.5
- proj_bias: float32 [4, 128], replicated, may hold values from -3 to 3
- prod_cot: bfloat16 [128, 960, 960], P('ch', 'row', 'col'), may hold values from -0.3984375 to 0.3984375
Outputs:
- grad_pair: bfloat16 [960, 960, 128], P(('row', 'ch'), 'col')
- grad_weight: float32 [128, 4, 128], replicated
- grad_bias: float32 [4, 128], replicated
- grad_gain: float32 [128], replicated
- grad_shift: float32 [128], replicated
All inputs are finite; a program needn't handle non-finite values.
Results may differ from a plain program's by a relative error of at most 0.015.
Values may be sent and summed in bfloat16 or wider, within the bound.
A program may use at most 192 MiB of HBM per device.

v0:
```python
import jax
import jax.numpy as jnp
from jax import lax
from jax.sharding import PartitionSpec as P

CROP = 960


EPSILON = 1e-05


def normalize(pair, norm_gain, norm_shift, proj_weight, proj_bias):
    values = pair.astype(jnp.float32)
    centred = values - jnp.mean(values, axis=-1, keepdims=True)
    inv_std = lax.rsqrt(jnp.mean(centred * centred, axis=-1, keepdims=True) + EPSILON)
    scaled = centred * inv_std
    normed = (scaled * norm_gain + norm_shift).astype(jnp.bfloat16)
    linear = jnp.einsum("ikf,fsc->isck", normed, proj_weight, preferred_element_type=jnp.float32)
    linear = linear + proj_bias[None, :, :, None]
    return (scaled, inv_std, normed, linear)


def norm_backward(normed_grad, scaled, inv_std, norm_gain):
    gained = normed_grad * norm_gain
    centre_term = jnp.mean(gained, axis=-1, keepdims=True)
    slope_term = jnp.mean(gained * scaled, axis=-1, keepdims=True)
    pair_grad = ((gained - centre_term - scaled * slope_term) * inv_std).astype(jnp.bfloat16)
    return (
        pair_grad,
        jnp.sum(normed_grad * scaled, axis=(0, 1)),
        jnp.sum(normed_grad, axis=(0, 1)),
    )


def shards(pair, norm_gain, norm_shift, proj_weight, proj_bias, prod_cot):
    scaled, inv_std, normed, linear = normalize(pair, norm_gain, norm_shift, proj_weight, proj_bias)
    gate_open = jax.nn.sigmoid(linear[:, 0::2])
    values_part = linear[:, 1::2]
    side_values = (gate_open * values_part).astype(jnp.bfloat16)
    tile_rows = pair.shape[0]
    tile_cols = pair.shape[1]
    hidden = proj_weight.shape[2]
    cot_rows = lax.all_gather(prod_cot, "col", axis=2, tiled=True)
    regrouped = lax.all_to_all(side_values, "ch", split_axis=2, concat_axis=0, tiled=True)
    left_part = regrouped[:, 0]
    right_part = regrouped[:, 1]
    cot_piece = cot_rows
    left_grad = jnp.einsum(
        "hij,jhk->ihk",
        cot_piece,
        lax.all_gather(right_part, "row", axis=0, tiled=True),
        preferred_element_type=jnp.float32,
    )
    left_grad = left_grad.astype(jnp.bfloat16)
    cot_piece = cot_rows
    right_grad = lax.psum_scatter(
        jnp.einsum("hij,ihk->jhk", cot_piece, left_part, preferred_element_type=jnp.float32).astype(
            jnp.bfloat16
        ),
        "row",
        scatter_dimension=0,
        tiled=True,
    )
    stacked = jnp.stack([left_grad, right_grad], axis=1)
    side_grad = lax.all_to_all(stacked, "ch", split_axis=0, concat_axis=2, tiled=True).astype(
        jnp.float32
    )
    gate_grad = side_grad * values_part * gate_open * (1.0 - gate_open)
    proj_grad = side_grad * gate_open
    linear_grad = jnp.stack([gate_grad, proj_grad], axis=2).reshape(tile_rows, 4, hidden, tile_cols)
    linear_grad = linear_grad.astype(jnp.bfloat16)
    normed_grad = jnp.einsum(
        "isck,fsc->ikf", linear_grad, proj_weight, preferred_element_type=jnp.float32
    )
    weight_part = jnp.einsum(
        "ikf,isck->fsc", normed, linear_grad, preferred_element_type=jnp.float32
    )
    bias_part = jnp.sum(linear_grad, axis=(0, 3), dtype=jnp.float32)
    inverse_crop = 1.0 / CROP
    weight_sum, bias_sum = lax.psum((weight_part, bias_part), ("row", "col", "ch"))
    grad_pair, gain_part, shift_part = norm_backward(normed_grad, scaled, inv_std, norm_gain)
    gain_sum, shift_sum = lax.psum((gain_part, shift_part), ("row", "col", "ch"))
    return (
        grad_pair,
        weight_sum * inverse_crop,
        bias_sum * inverse_crop,
        gain_sum * inverse_crop,
        shift_sum * inverse_crop,
    )


def solution(mesh):
    in_specs = (P(("row", "ch"), "col", None), P(), P(), P(), P(), P("ch", "row", "col"))
    out_specs = (P(("row", "ch"), "col", None), P(), P(), P(), P())
    return jax.shard_map(shards, mesh=mesh, in_specs=in_specs, out_specs=out_specs, check_vma=False)
```

profile of v0, /device:TPU:1, one launch (start us, length us, event | category | flops | bytes accessed | tf_op | source)
XLA Modules:
  0.0 740.2 jit_solution(2074416117005942401)
XLA Ops:
  7.2 4.4 copy.52
  16.8 5.1 copy-done
  25.1 10.9 %copy.48 = bf16[30,2,128,240]{3,1,0,2:T(2,128)(2,1)} copy(bf16[30,2,128,240]{2,3,1,0:T(8,128)(2,1)} %multiply_convert_fusion) | data formatting | bytes 7372800 | tf_op jit(solution)/shard_map/convert_element_type | solution.py:39
  36.0 52.5 %all_to_all.27 = bf16[30,2,128,240]{3,1,0,2:T(2,128)(2,1)S(1)} all-to-all(bf16[30,2,128,240]{3,1,0,2:T(2,128)(2,1)} %copy.48), channel_id=1, replica_groups=mesh['row'=8,'col'=4,'ch'=4] {'ch'}, dimensions={2} | all-to-all | bytes 7372800 | tf_op jit(solution)/shard_map/all_to_all | solution.py:44
  92.4 4.5 copy.72
  97.0 12.2 %copy.53 = bf16[32,120,960]{2,1,0:T(8,128)(2,1)} copy(bf16[32,120,960]{1,0,2:T(8,128)(2,1)} %all-gather.4.cloned.1.call-done) | data formatting | bytes 14745600 | tf_op jit(solution)/shard_map/all_gather | solution.py:43
  109.2 13.6 %convolution_convert_fusion = bf16[32,240,960]{2,1,0:T(8,128)(2,1)} fusion(bf16[32,120,960]{2,1,0:T(8,128)(2,1)} %copy.53, bf16[120,1,32,240]{0,3,2,1:T(8,128)(2,1)} %copy.72), kind=kOutput, calls=%fused_computation.5 | convolution fusion | flops 1776844800 | bytes 23961600 | tf_op jit(solution)/shard_map/hij,ihk->jhk/dot_general | solution.py:57
  122.8 19.4 %copy.70 = bf16[960,7680]{1,0:T(8,128)(2,1)} copy(bf16[960,7680]{0,1:T(8,128)(2,1)} %bitcast.72) | data formatting | bytes 29491200
  142.3 114.9 %all-gather.6.cloned.1.call-done = bf16[960,1,32,240]{3,2,1,0:T(8,128)(2,1)} async-done(((bf16[120,1,32,240]{3,2,1,0:T(8,128)(2,1)}), bf16[960,1,32,240]{3,2,1,0:T(8,128)(2,1)}) %all-gather.6.cloned.1.call-update) | async-done | bytes 14745616 | tf_op jit(solution)/shard_map/all_gather | solution.py:51
  257.1 23.0 %copy.51 = bf16[960,1,32,240]{0,3,2,1:T(8,128)(2,1)} copy(bf16[960,1,32,240]{3,2,1,0:T(8,128)(2,1)} %all-gather.6.cloned.1.call-done) | data formatting | bytes 29491200 | tf_op jit(solution)/shard_map/all_gather | solution.py:51
  280.1 11.1 %convert_bitcast_fusion.1 = bf16[120,1,32,240]{0,3,2,1:T(8,128)(2,1)} fusion(bf16[32,120,960]{2,1,0:T(8,128)(2,1)} %copy.53, bf16[960,1,32,240]{0,3,2,1:T(8,128)(2,1)} %copy.51), kind=kOutput, calls=%fused_computation.32 | convolution fusion | flops 1770393600 | bytes 23961600 | tf_op jit(solution)/shard_map/hij,jhk->ihk/dot_general | solution.py:48
  291.2 120.0 %reduce-scatter.4.cloned.1.call-done = bf16[120,7680]{1,0:T(8,128)(2,1)} async-done(((bf16[960,7680]{1,0:T(8,128)(2,1)}), bf16[120,7680]{1,0:T(8,128)(2,1)}) %reduce-scatter.4.cloned.1.call-update) | async-done | bytes 1843216
  415.0 4.9 pad_maximum_fusion
  419.9 7.8 %copy.56 = bf16[120,2,32,240]{3,2,1,0:T(8,128)(2,1)} copy(bf16[120,2,32,240]{0,3,2,1:T(8,128)(2,1)} %pad_maximum_fusion) | data formatting | bytes 7372800 | tf_op jit(solution)/shard_map/stack | solution.py:64
  427.7 50.6 %all_to_all.28 = bf16[120,2,32,240]{3,2,1,0:T(8,128)(2,1)S(1)} all-to-all(bf16[120,2,32,240]{3,2,1,0:T(8,128)(2,1)} %copy.56), channel_id=1, replica_groups=mesh['row'=8,'col'=4,'ch'=4] {'ch'}, dimensions={0} | all-to-all | bytes 7372800 | tf_op jit(solution)/shard_map/all_to_all | solution.py:65
  483.2 8.9 %copy.58 = f32[30,2,128,240]{2,3,1,0:T(8,128)} copy(f32[30,2,128,240]{3,2,1,0:T(8,128)} %bitcast.73) | data formatting | bytes 14745600 | tf_op jit(solution)/shard_map/convert_element_type | solution.py:65
  492.1 11.9 %multiply_bitcast_fusion.1 = (bf16[30,2,1,128,240]{3,4,1,0,2:T(8,128)(2,1)}, bf16[30,2,1,128,240]{3,4,1,0,2:T(8,128)(2,1)}) fusion(f32[30,2,128,240]{2,3,1,0:T(8,128)} %copy.58, f32[30,4,128,240]{2,3,1,0:T(8,128)} %copy-done), kind=kLoop, calls=%fused_computation.8 | loop fusion | flops 18432000 | bytes 29491200 | tf_op jit(solution)/shard_map/stack | solution.py:70
  504.0 5.1 convert_reduce_fusion
  509.1 3.9 copy.60
  513.0 8.3 %convolution_bitcast_fusion = f32[128,4,128]{2,0,1:T(8,128)} fusion(bf16[30,4,128,240]{2,3,1,0:T(8,128)(2,1)} %bitcast.78, bf16[30,240,128]{2,1,0:T(8,128)(2,1)S(1)} %copy-done.1, f32[128]{0:T(128)S(1)} %copy-done.5, f32[128]{0:T(128)S(1)} %copy-done.4, f32[30,240]{1,0:T(8,128)S(1)} %add_rsqrt_fusion, f32[30,240]{1,0:T(8,128)S(1)} %broadcast_multiply_fusion.3), kind=kOutput, calls=%fused_computation.34 | convolution fusion | flops 949248000 | bytes 9536768 | tf_op jit(solution)/shard_map/ikf,isck->fsc/dot_general | solution.py:75
  521.3 7.5 %fusion.14 = (f32[128]{0:T(128)S(1)}, f32[30,240]{1,0:T(8,128)S(1)}, f32[30,240]{1,0:T(8,128)S(1)}, f32[128]{0:T(128)S(1)}, f32[30,240,128,1]{2,1,3,0:T(8,128)}) fusion(bf16[30,240,128]{2,1,0:T(8,128)(2,1)S(1)} %copy-done.1, f32[30,240]{1,0:T(8,128)S(1)} %add_rsqrt_fusion, f32[30,240]{1,0:T(8,128)S(1)} %broadcast_multiply_fusion.3, f32[128]{0:T(128)S(1)} %copy-done.4, ...), kind=kOutput, calls=%fused_computation.26 | convolution fusion | flops 952919808 | bytes 13150208 | tf_op jit(solution)/shard_map/isck,fsc->ikf/dot_general | solution.py:72
  528.7 64.4 %all-reduce = (f32[4,128]{1,0:T(4,128)S(1)}, f32[128]{0:T(128)S(1)}, f32[128]{0:T(128)S(1)}) all-reduce(f32[4,128]{1,0:T(4,128)S(1)} %bitcast.80, f32[128]{0:T(128)S(1)} %get-tuple-element.25, f32[128]{0:T(128)S(1)} %get-tuple-element.28), channel_id=1, replica_groups=mesh['row'=8,'col'=4,'ch'=4] {'row','col','ch'}, use_global_device_ids=true, to_apply=%region_7.0 | all-reduce | flops 768 | bytes 6144 | tf_op jit(solution)/shard_map/psum | solution.py:80
  593.8 8.9 %fusion.13 = bf16[30,240,128]{2,1,0:T(8,128)(2,1)} fusion(bf16[30,240,128]{2,1,0:T(8,128)(2,1)S(1)} %copy-done.1, f32[30,240,128,1]{2,1,3,0:T(8,128)} %get-tuple-element.38, f32[30,240]{1,0:T(8,128)S(1)} %get-tuple-element.39, f32[30,240]{1,0:T(8,128)S(1)} %get-tuple-element.40, f32[128]{0:T(128)S(1)} %copy-done.4, f32[30,240]{1,0:T(8,128)S(1)} %add_rsqrt_fusion, ...), kind=kLoop, calls=%fused_computation.25 | loop fusion | flops 8294400 | bytes 7488512 | tf_op jit(solution)/shard_map/convert_element_type | solution.py:27
  603.2 128.6 %all-reduce.3.cloned.1.call-done = f32[128,4,128]{2,0,1:T(8,128)} async-done(((f32[128,4,128]{2,0,1:T(8,128)}), f32[128,4,128]{2,0,1:T(8,128)}) %all-reduce.3.cloned.1.call-update) | async-done | bytes 262160 | tf_op jit(solution)/shard_map/psum | solution.py:80
  (38 shorter events, 24.1 us)
Async XLA Ops:
  7.2 4.5 copy-start.1
  7.2 89.8 %all-gather.4.cloned.1.call-start = ((), (), s32[]{:S(2)}) async-start(), calls=%async_computation.3 | async-start | bytes 9830400 | tf_op jit(solution)/shard_map/all_gather | solution.py:43
  11.6 3.0 copy-start.2
  11.6 3.0 copy-start.3
  11.6 3.0 copy-start.4
  11.6 3.0 copy-start.5
  11.6 245.5 %all-gather.6.cloned.1.call-start = ((), (), s32[]{:S(2)}) async-start(), calls=%async_computation.5 | async-start | bytes 17694720 | tf_op jit(solution)/shard_map/all_gather | solution.py:51
  16.8 5.1 copy-start
  92.2 318.9 %reduce-scatter.4.cloned.1.call-start = ((), (), s32[]{:S(2)}) async-start(), calls=%async_computation.6 | async-start | bytes 16588800
  142.2 589.7 %all-reduce.3.cloned.1.call-start = ((), (), s32[]{:S(2)}) async-start(), calls=%async_computation.4 | async-start | bytes 524288 | tf_op jit(solution)/shard_map/psum | solution.py:80
Sparse Core Ops, SparseCore 0:
  11.8 81.8 all-gather.3
  95.4 161.7 all-gather.5
  259.5 151.5 reduce-scatter.3
  593.9 137.9 all-reduce.2
where the time goes:
time: 743 us; the launch traced here: 740 us
  waiting for transfers between devices  364 us (49%)
  blocking collectives  167 us (22%)
  local copies, waits for them, and re-layouts  112 us (15%)
  matrix products  42.6 us (6%)
  other arithmetic  40 us (5%)
  between operations  13.9 us (2%)
    psum x1, waiting for transfers between devices, shards(): lax.psum((weight_part, bias_part), ('row', 'col', 'ch'))  129 us
    unnamed x5, waiting for transfers between devices  120 us
    all_gather x1, waiting for transfers between devices, shards(): lax.all_gather(right_part, 'row', axis=0, tiled=True)  115 us
    psum x1, blocking collectives, shards(): lax.psum((weight_part, bias_part), ('row', 'col', 'ch'))  64.4 us
    all_to_all x1, blocking collectives, shards(): lax.all_to_all(side_values, 'ch', split_axis=2, concat_axis=0, tiled=True)  52.5 us
    all_to_all x1, blocking collectives, shards(): lax.all_to_all(stacked, 'ch', split_axis=0, concat_axis=2, tiled=True)  50.6 us
    unnamed x17, local copies, waits for them, and re-layouts  38.2 us
    all_gather x1, local copies, waits for them, and re-layouts, shards(): lax.all_gather(right_part, 'row', axis=0, tiled=True)  23 us
  transfers between devices with their start and end apart: 4, of which 3 were waited for; matrix products, arithmetic and copies ran while one was open for 16% of the time, Pallas kernels for 0%

commit v1 on v0

v1 whole, which is shorter than its diff:
```python
import functools

import jax
import jax.numpy as jnp
from jax import lax
from jax.experimental import pallas as pl
from jax.experimental.pallas import tpu as pltpu
from jax.sharding import PartitionSpec as P

MESH = pl.DeviceIdType.MESH
EPSILON = 1e-05
CROP = 960
ROWS = 30
COLS = 240
PAIRS = ROWS // 2
HALF_COLS = (128, COLS - 128)
OWNERS = 32
F32, BF16 = jnp.float32, jnp.bfloat16

STEPS = (
    (2, 2),
    (1, 1), (3, 3), (1, 3), (3, 1),
    (1, 2), (2, 1), (3, 2), (2, 3),
    (2, 0), (0, 2),
    (1, 0), (0, 1), (3, 0), (0, 3),
)
OFFSETS = []
for start in range(0, len(STEPS), 1):
    OFFSETS.append((*STEPS[start], 0))
    OFFSETS.append((*STEPS[start], 1))
OFFSETS.append((0, 0, 1))


def kernel(
    pair_ref, cot_ref, wt_ref, wb_ref, bias_ref, gain_ref, shift_ref,
    grad_ref, dw_ref, gs_ref,
    stage, cotf, send1, recv1, left, right, wide, send2, recv2, scaled_s, inv_s, normed_s, acc_gain, acc_shift,
    cs, cr, xs, xr, fs, fr, s1, r1, s2, r2,
):
    row, col, ch = lax.axis_index("row"), lax.axis_index("col"), lax.axis_index("ch")
    me = row * 4 + ch
    z = (ch // 2) * 2 + row // 4
    y = row % 4
    core = ch % 2
    east, west = (col + 1) % 4, (col + 3) % 4

    partners = []
    for dz, dy, dk in OFFSETS:
        z2, y2, k2 = (z + dz) % 4, (y + dy) % 4, (core + dk) % 2
        partners.append(((z2 % 2) * 4 + y2, (z2 // 2) * 2 + k2))

    barrier = pltpu.get_barrier_semaphore()
    for r, g in partners:
        pl.semaphore_signal(barrier, 1, device_id=(r, col, g), device_id_type=MESH)
    for c in (east, west):
        pl.semaphore_signal(barrier, 1, device_id=(row, c, ch), device_id_type=MESH)

    def stage_one(c, carry):
        stage[c] = jnp.zeros((128, 256), BF16)
        stage[c, 0:120, 0:COLS] = cot_ref[c]
        return carry

    lax.fori_loop(0, 32, stage_one, 0)
    pl.semaphore_wait(barrier, len(partners) + 2)

    def cot_copy(c, there):
        return pltpu.make_async_remote_copy(
            src_ref=stage.at[there * 4 + c],
            dst_ref=cotf.at[c, col, pl.ds(row * 128, 128)],
            send_sem=cs.at[c, there], recv_sem=cr.at[c, row],
            device_id=(there, col, ch), device_id_type=MESH,
        )

    def cot_arrival(c, source):
        return pltpu.make_async_remote_copy(
            src_ref=stage.at[c],
            dst_ref=cotf.at[c, col, pl.ds(source * 128, 128)],
            send_sem=cs.at[c, source], recv_sem=cr.at[c, source],
            device_id=(row, col, ch), device_id_type=MESH,
        )

    for c in range(4):
        for step in (6, 5, 7, 2, 4, 1, 3):
            there = ((row // 4 + step // 4) % 2) * 4 + (row + step) % 4
            cot_copy(c, there).start()
        cotf[c, col, pl.ds(row * 128, 128)] = stage[row * 4 + c]

    for c in range(4):
        for b in range(8):
            left[c, b * 128 + 112:(b + 1) * 128] = jnp.zeros((16, 128), BF16)
        for b in range(4):
            right[c, b * 256 + COLS:(b + 1) * 256] = jnp.zeros((16, 128), BF16)
    dw_ref[...] = jnp.zeros_like(dw_ref)
    acc_gain[...] = jnp.zeros_like(acc_gain)
    acc_shift[...] = jnp.zeros_like(acc_shift)

    def forward(kh, ip, carry):
        width = HALF_COLS[kh]
        tokens = []
        for half in range(2):
            x = pair_ref[2 * ip + half, kh * 128:kh * 128 + width].astype(F32)
            if width < 128:
                x = jnp.concatenate([x, jnp.zeros((128 - width, 128), F32)], axis=0)
            tokens.append(x.T)
        x = jnp.concatenate(tokens, axis=1)
        centred = x - jnp.mean(x, axis=0, keepdims=True)
        inv_std = lax.rsqrt(jnp.mean(centred * centred, axis=0, keepdims=True) + EPSILON)
        scaled = centred * inv_std
        normed = (scaled * gain_ref[...] + shift_ref[...]).astype(BF16)
        slot = kh * PAIRS + ip
        scaled_s[slot] = scaled
        inv_s[slot] = inv_std
        normed_s[slot, 0:128] = normed
        normed_s[slot, 128:144] = jnp.ones((16, 256), BF16)
        linear = jnp.dot(wt_ref[...], normed, preferred_element_type=F32) + bias_ref[...]
        gate = 0.5 * jnp.tanh(0.5 * linear[0:256]) + 0.5
        side = gate * linear[256:512]
        if width < 128:
            lane = lax.broadcasted_iota(jnp.int32, (256, 256), 1)
            side = jnp.where(lane % 128 < width, side, 0.0)
        packed = jnp.concatenate(
            [side[:, 0:128].reshape(OWNERS, 8, 128), side[:, 128:256].reshape(OWNERS, 8, 128)], axis=1
        ).astype(BF16)
        send1[kh, :, pl.ds(pl.multiple_of(ip * 16, 16), 16), :] = packed
        return carry

    def exchange(source, target, send_sem, recv_sem, kh, there_r, there_g):
        there = there_r * 4 + there_g
        return pltpu.make_async_remote_copy(
            src_ref=source.at[kh, there], dst_ref=target.at[kh, me],
            send_sem=send_sem.at[kh, there], recv_sem=recv_sem.at[kh, me],
            device_id=(there_r, col, there_g), device_id_type=MESH,
        )

    def arrival(source, target, send_sem, recv_sem, kh, there):
        return pltpu.make_async_remote_copy(
            src_ref=source.at[kh, there], dst_ref=target.at[kh, there],
            send_sem=send_sem.at[kh, there], recv_sem=recv_sem.at[kh, there],
            device_id=(row, col, ch), device_id_type=MESH,
        )

    def send_all(source, target, send_sem, recv_sem, kh):
        for r, g in partners:
            exchange(source, target, send_sem, recv_sem, kh, r, g).start()
        target[kh, me] = source[kh, me]

    def others(action):
        def one(there, carry):
            @pl.when(there != me)
            def _():
                action(there)
            return carry

        lax.fori_loop(0, OWNERS, one, 0)

    def x_copy(c, block, part, sems, recvs, side, there):
        return pltpu.make_async_remote_copy(
            src_ref=cotf.at[c, block, part], dst_ref=cotf.at[c, block, part],
            send_sem=sems.at[c, side], recv_sem=recvs.at[c, side],
            device_id=(row, there, ch), device_id_type=MESH,
        )

    WHOLE, LOW, HIGH = pl.ds(0, 1024), pl.ds(0, 512), pl.ds(512, 512)
    far = (col + 2) % 4

    def x_send(c):
        def one(source, carry):
            @pl.when(source != row)
            def _():
                cot_arrival(c, source).wait_recv()
            return carry

        lax.fori_loop(0, 8, one, 0)
        x_copy(c, col, WHOLE, xs, xr, 0, east).start()
        x_copy(c, col, WHOLE, xs, xr, 1, west).start()

    def x_forward(c):
        x_copy(c, west, WHOLE, xs, xr, 0, east).wait_recv()
        x_copy(c, west, LOW, fs, fr, 0, east).start()
        x_copy(c, east, WHOLE, xs, xr, 1, west).wait_recv()
        x_copy(c, east, HIGH, fs, fr, 1, west).start()

    def x_finish(c):
        x_copy(c, far, LOW, fs, fr, 0, east).wait_recv()
        x_copy(c, far, HIGH, fs, fr, 1, west).wait_recv()

    def regroup(kh):
        others(lambda there: arrival(send1, recv1, s1, r1, kh, there).wait_recv())

        def widen(source, carry):
            wide[pl.ds(pl.multiple_of(source * 240, 8), 240)] = recv1[kh, source].astype(F32)
            return carry

        lax.fori_loop(0, OWNERS, widen, 0)
        for c in range(4):
            for b in range(8):
                left[c, b * 128:b * 128 + 120] = wide[pl.ds(b * 960 + c, 120, stride=8)].astype(BF16)
            for b in range(4):
                right[c, b * 256:b * 256 + COLS] = wide[pl.ds(b * 1920 + 4 + c, COLS, stride=8)].astype(BF16)

    def triangle(c):
        for b in range(8):
            rows = pl.ds(b * 128, 128)
            total = jnp.zeros((128, 128), F32)
            for x in range(4):
                total += jnp.dot(cotf[c, x, rows], right[c, x * 256:(x + 1) * 256], preferred_element_type=F32)
            wide[pl.ds(b * 960 + c, 120, stride=8)] = total[0:120]
        for x in range(4):
            total = lax.dot_general(
                cotf[c, x], left[c], (((0,), (0,)), ((), ())), preferred_element_type=F32
            )
            wide[pl.ds(x * 1920 + 4 + c, COLS, stride=8)] = total[0:COLS]

    def give_back(kh):
        def narrow(target, carry):
            send2[kh, target] = wide[pl.ds(pl.multiple_of(target * 240, 8), 240)].astype(BF16)
            return carry

        lax.fori_loop(0, OWNERS, narrow, 0)
        send_all(send2, recv2, s2, r2, kh)

    def backward(kh, ip, carry):
        width = HALF_COLS[kh]
        slot = kh * PAIRS + ip
        back = recv2[kh, :, pl.ds(pl.multiple_of(ip * 16, 16), 16), :].astype(F32)
        side_grad = jnp.concatenate(
            [back[:, 0:8].reshape(256, 128), back[:, 8:16].reshape(256, 128)], axis=1
        )
        normed = normed_s[slot, 0:128]
        linear = jnp.dot(wt_ref[...], normed, preferred_element_type=F32) + bias_ref[...]
        gate = 0.5 * jnp.tanh(0.5 * linear[0:256]) + 0.5
        value_grad = side_grad * gate
        gate_grad = value_grad * linear[256:512] * (1.0 - gate)
        linear_grad = jnp.concatenate([gate_grad.astype(BF16), value_grad.astype(BF16)], axis=0)
        normed_grad = jnp.dot(wb_ref[...], linear_grad, preferred_element_type=F32)
        dw_ref[...] += lax.dot_general(
            linear_grad, normed_s[slot], (((1,), (1,)), ((), ())), preferred_element_type=F32
        )
        scaled = scaled_s[slot]
        acc_gain[...] += normed_grad * scaled
        acc_shift[...] += normed_grad
        gained = normed_grad * gain_ref[...]
        centre = jnp.mean(gained, axis=0, keepdims=True)
        slope = jnp.mean(gained * scaled, axis=0, keepdims=True)
        result = (gained - centre - scaled * slope) * inv_s[slot]
        for half in range(2):
            out = result[:, half * 128:(half + 1) * 128].T.astype(BF16)
            grad_ref[2 * ip + half, kh * 128:kh * 128 + width] = out[0:width]
        return carry

    lax.fori_loop(0, PAIRS, functools.partial(forward, 0), 0)
    send_all(send1, recv1, s1, r1, 0)
    x_send(0)
    lax.fori_loop(0, 8, functools.partial(forward, 1), 0)
    x_send(1)
    lax.fori_loop(8, PAIRS, functools.partial(forward, 1), 0)
    send_all(send1, recv1, s1, r1, 1)
    x_send(2)
    x_forward(0)
    x_send(3)
    x_forward(1)
    regroup(0)
    x_forward(2)
    x_finish(0)
    triangle(0)
    x_forward(3)
    for c in range(1, 4):
        x_finish(c)
        triangle(c)
    give_back(0)
    regroup(1)
    for c in range(4):
        triangle(c)
    give_back(1)
    for kh in range(2):
        others(lambda there: arrival(send2, recv2, s2, r2, kh, there).wait_recv())
        lax.fori_loop(0, PAIRS, functools.partial(backward, kh), 0)
    gs_ref[0] = jnp.sum(acc_gain[...].T, axis=0, keepdims=True)
    gs_ref[1] = jnp.sum(acc_shift[...].T, axis=0, keepdims=True)

    for c in range(4):
        def sent(there, carry):
            @pl.when(there != row)
            def _():
                cot_copy(c, there).wait_send()
            return carry

        lax.fori_loop(0, 8, sent, 0)
        x_copy(c, col, WHOLE, xs, xr, 0, east).wait_send()
        x_copy(c, col, WHOLE, xs, xr, 1, west).wait_send()
        x_copy(c, west, LOW, fs, fr, 0, east).wait_send()
        x_copy(c, east, HIGH, fs, fr, 1, west).wait_send()
    for kh in range(2):
        others(lambda there: arrival(send1, recv1, s1, r1, kh, there).wait_send())
        others(lambda there: arrival(send2, recv2, s2, r2, kh, there).wait_send())


def by_owner(array):
    lead = array.shape[:-2]
    n = len(lead)
    parts = array.reshape(*lead, 2, 2, 4, 8, 4)
    axes = tuple(range(n)) + tuple(n + a for a in (1, 3, 2, 0, 4))
    return parts.transpose(axes).reshape(*lead, 512)


def by_stream(array):
    lead = array.shape[:-1]
    n = len(lead)
    parts = array.reshape(*lead, 2, 8, 4, 2, 4)
    axes = tuple(range(n)) + tuple(n + a for a in (3, 0, 2, 1, 4))
    return parts.transpose(axes).reshape(*lead, 4, 128)


def shards(pair, norm_gain, norm_shift, proj_weight, proj_bias, prod_cot):
    wb = by_owner(proj_weight)
    wt = wb.T
    bias = jnp.broadcast_to(by_owner(proj_bias)[:, None], (512, 256))
    gain = jnp.broadcast_to(norm_gain[:, None], (128, 256))
    shift = jnp.broadcast_to(norm_shift[:, None], (128, 256))
    vmem = pl.BlockSpec(memory_space=pltpu.VMEM)
    dma = pltpu.SemaphoreType.DMA
    grad_pair, dw, gs = pl.pallas_call(
        kernel,
        out_shape=(
            jax.ShapeDtypeStruct((ROWS, COLS, 128), BF16),
            jax.ShapeDtypeStruct((512, 144), F32),
            jax.ShapeDtypeStruct((2, 1, 128), F32),
        ),
        in_specs=[vmem] * 7,
        out_specs=(vmem,) * 3,
        scratch_shapes=[
            pltpu.VMEM((32, 128, 256), BF16),
            pltpu.VMEM((4, 4, 1024, 256), BF16),
            pltpu.VMEM((2, OWNERS, 240, 128), BF16),
            pltpu.VMEM((2, OWNERS, 240, 128), BF16),
            pltpu.VMEM((4, 1024, 128), BF16),
            pltpu.VMEM((4, 1024, 128), BF16),
            pltpu.VMEM((CROP * 8, 128), F32),
            pltpu.VMEM((2, OWNERS, 240, 128), BF16),
            pltpu.VMEM((2, OWNERS, 240, 128), BF16),
            pltpu.VMEM((2 * PAIRS, 128, 256), F32),
            pltpu.VMEM((2 * PAIRS, 1, 256), F32),
            pltpu.VMEM((2 * PAIRS, 144, 256), BF16),
            pltpu.VMEM((128, 256), F32),
            pltpu.VMEM((128, 256), F32),
            dma((4, 8)), dma((4, 8)), dma((4, 2)), dma((4, 2)), dma((4, 2)), dma((4, 2)),
            dma((2, OWNERS)), dma((2, OWNERS)), dma((2, OWNERS)), dma((2, OWNERS)),
        ],
        compiler_params=pltpu.CompilerParams(
            collective_id=0, has_side_effects=True, vmem_limit_bytes=60 << 20
        ),
        name="triangle_backward",
    )(pair, prod_cot, wt, wb, bias, gain, shift)
    sums = jnp.concatenate(
        [dw[:, 0:128], dw[:, 128].reshape(4, 128), gs.reshape(2, 128)], axis=0
    )
    sums = lax.psum(sums, ("row", "col", "ch")) * (1.0 / CROP)
    grad_weight = by_stream(sums[0:512].T)
    grad_bias = by_stream(sums[512:516].reshape(512))
    return grad_pair, grad_weight, grad_bias, sums[516], sums[517]


def solution(mesh):
    in_specs = (P(("row", "ch"), "col", None), P(), P(), P(), P(), P("ch", "row", "col"))
    out_specs = (P(("row", "ch"), "col", None), P(), P(), P(), P())
    return jax.shard_map(shards, mesh=mesh, in_specs=in_specs, out_specs=out_specs, check_vma=False)
```

time: 743 us -> 320 us (0.43)
  waiting for transfers between devices: 364 us -> 143 us
  blocking collectives: 167 us -> 0 us
  Pallas kernels: 0 us -> 148 us
  local copies, waits for them, and re-layouts: 112 us -> 12.3 us
  matrix products: 42.6 us -> 0 us
  other arithmetic: 40 us -> 2.38 us
    pallas_call x0 -> x1, Pallas kernels: none -> 148 us  [shards(): pl.pallas_call(kernel, out_shape=(jax.ShapeDtypeStruct((ROWS, COLS, 128),...]
    unnamed x5 -> x1, waiting for transfers between devices: 120 us -> 0.02 us
    all_gather x2 -> x0, waiting for transfers between devices: 115 us -> none  [the longest x1 115 us: shards(): lax.all_gather(right_part, 'row', axis=0, tiled=True)]
    all_to_all x2 -> x0, blocking collectives: 103 us -> none  [the longest x1 52.5 us: shards(): lax.all_to_all(side_values, 'ch', split_axis=2, concat_axis=0, tiled=True)]
    psum x1 -> x0, blocking collectives: 64.4 us -> none  [shards(): lax.psum((weight_part, bias_part), ('row', 'col', 'ch'))]
    dot_general x5 -> x0, matrix products: 42.6 us -> none  [the longest x1 13.6 us: shards(): jnp.einsum('hij,ihk->jhk', cot_piece, left_part, preferred_element_type=j...]
    all_gather x2 -> x0, local copies, waits for them, and re-layouts: 35.2 us -> none  [the longest x1 23 us: shards(): lax.all_gather(right_part, 'row', axis=0, tiled=True)]
    unnamed x17 -> x7, local copies, waits for them, and re-layouts: 38.2 us -> 3.11 us
  transfers between devices with their start and end apart: 4 -> 1, of which waited for: 3 -> 1; matrix products, arithmetic and copies ran while one was open for 16% -> 0% of each run, Pallas kernels for 0% -> 0%
where the time goes in v1:
time: 320 us
  Pallas kernels  148 us (46%)
  waiting for transfers between devices  143 us (45%)
  between operations  14.1 us (4%)
  local copies, waits for them, and re-layouts  12.3 us (4%)
    pallas_call x1, Pallas kernels, shards(): pl.pallas_call(kernel, out_shape=(jax.ShapeDtypeStruct((ROWS, COLS, 128),...  148 us
    psum x1, waiting for transfers between devices, shards(): sums = lax.psum(sums, ('row', 'col', 'ch')) * (1.0 / CROP)  143 us
  transfers between devices with their start and end apart: 1, of which 1 were waited for; matrix products, arithmetic and copies ran while one was open for 0% of the time, Pallas kernels for 0%

profile of v1, /device:TPU:1, one launch (start us, length us, event | category | flops | bytes accessed | tf_op | source)
XLA Modules:
  0.0 319.8 jit_solution(8887347808029626641)
XLA Ops:
  7.2 0.0 all-reduce.2.cloned.1.call-start
  7.2 1.0 copy.15
  8.3 0.0 copy-start.1
  8.3 0.8 copy.18.wb_ref
  9.1 0.8 reshape.36
  9.9 0.1 copy.17
  9.9 0.1 broadcast_in_dim.8
  10.1 0.9 broadcast_in_dim.9.bias_ref
  11.0 1.4 broadcast_in_dim.10.gain_ref
  12.4 1.4 broadcast_in_dim.22.shift_ref
  13.8 0.0 copy-done.1
  13.8 148.4 %triangle_backward.1 = (bf16[30,240,128]{2,1,0:T(8,128)(2,1)}, f32[512,144]{1,0:T(8,128)}, f32[2,1,128]{2,1,0:T(1,128)}) custom-call(bf16[30,240,128]{2,1,0:T(8,128)(2,1)} %pair_ref.1, bf16[32,120,240]{2,1,0:T(8,128)(2,1)} %cot_ref.1, bf16[512,128]{1,0:T(8,128)(2,1)} %bitcast.23, bf16[128,512]{1,0:T(8,128)(2,1)} %copy.18.wb_ref, ...), custom_call_target="tpu_custom_call" | custom-call | tf_op jit(solution)/shard_map/triangle_backward/pallas_call | solution.py:322
  162.2 1.0 slice.18
  163.2 1.2 slice_reduce_fusion
  164.5 1.4 pad_maximum_fusion
  165.9 0.0 all-reduce.2.cloned.1.call-update
  165.9 142.5 %all-reduce.2.cloned.1.call-done = f32[518,128]{1,0:T(8,128)} async-done(((f32[518,128]{1,0:T(8,128)}), f32[518,128]{1,0:T(8,128)}) %all-reduce.2.cloned.1.call-update) | async-done | bytes 265232 | tf_op jit(solution)/shard_map/psum | solution.py:357
  308.4 1.0 broadcast_multiply_fusion
  309.4 0.5 slice_bitcast_fusion
  309.9 0.1 copy.19
  310.0 0.8 copy.21
  310.8 0.1 reshape_reshape.3
  311.0 0.7 reshape.40
  311.7 1.2 copy.24
  (6 shorter events, 0.1 us)
Async XLA Ops:
  7.2 301.2 %all-reduce.2.cloned.1.call-start = ((), (), s32[]{:S(2)}) async-start(), calls=%async_computation | async-start | bytes 532480 | tf_op jit(solution)/shard_map/psum | solution.py:357
  8.3 5.5 %copy-start.1 = (bf16[128,2,8,4,2,4]{0,5,4,3,2,1:T(4,128)(2,1)}, bf16[128,2,8,4,2,4]{0,5,4,3,2,1:T(4,128)(2,1)S(1)}, u32[]{:S(2)}) copy-start(bf16[128,2,8,4,2,4]{0,5,4,3,2,1:T(4,128)(2,1)S(1)} %copy.16) | copy-start | bytes 393220
  163.2 148.5 %copy-start = (bf16[30,240,128]{2,1,0:T(8,128)(2,1)S(1)}, bf16[30,240,128]{2,1,0:T(8,128)(2,1)}, u32[]{:S(2)}) copy-start(bf16[30,240,128]{2,1,0:T(8,128)(2,1)} %get-tuple-element.23) | copy-start | bytes 5529604
Sparse Core Ops, SparseCore 0:
  166.0 142.3 all-reduce.1

commit v2 on v1

--- a/solution.py
+++ b/solution.py
@@ -31,18 +31,30 @@
 OFFSETS.append((0, 0, 1))
 
 
+GROUPS = [(kind, t, side) for kind in range(2) for t in range(OWNERS) for side in range(2)]
+
+
+def owner_row(kind, t, side):
+    return kind * 256 + t * 8 + side * 4
+
+
+def stream_row(kind, t, side):
+    return (side * 2 + kind) * 128 + (t % 4) * 32 + (t // 4) * 4
+
+
 def kernel(
-    pair_ref, cot_ref, wt_ref, wb_ref, bias_ref, gain_ref, shift_ref,
-    grad_ref, dw_ref, gs_ref,
+    pair_ref, cot_ref, weight_ref, biases_ref, norm_ref,
+    grad_ref, dw_ref, small_ref,
     stage, cotf, send1, recv1, left, right, wide, send2, recv2, scaled_s, inv_s, normed_s, acc_gain, acc_shift,
-    cs, cr, xs, xr, fs, fr, s1, r1, s2, r2,
+    wt_ref, wb_ref, bias_ref, gain_ref, shift_ref, natural, owned, acc, small, part_s, part_r, line, whole,
+    cs, cr, xs, xr, fs, fr, s1, r1, s2, r2, as_, ar, bs, br, gs_, gr,
 ):
     row, col, ch = lax.axis_index("row"), lax.axis_index("col"), lax.axis_index("ch")
     me = row * 4 + ch
     z = (ch // 2) * 2 + row // 4
     y = row % 4
     core = ch % 2
-    east, west = (col + 1) % 4, (col + 3) % 4
+    east, west, far = (col + 1) % 4, (col + 3) % 4, (col + 2) % 4
 
     partners = []
     for dz, dy, dk in OFFSETS:
@@ -52,7 +64,7 @@
     barrier = pltpu.get_barrier_semaphore()
     for r, g in partners:
         pl.semaphore_signal(barrier, 1, device_id=(r, col, g), device_id_type=MESH)
-    for c in (east, west):
+    for c in (east, west, far):
         pl.semaphore_signal(barrier, 1, device_id=(row, c, ch), device_id_type=MESH)
 
     def stage_one(c, carry):
@@ -61,7 +73,7 @@
         return carry
 
     lax.fori_loop(0, 32, stage_one, 0)
-    pl.semaphore_wait(barrier, len(partners) + 2)
+    pl.semaphore_wait(barrier, len(partners) + 3)
 
     def cot_copy(c, there):
         return pltpu.make_async_remote_copy(
@@ -85,12 +97,40 @@
             cot_copy(c, there).start()
         cotf[c, col, pl.ds(row * 128, 128)] = stage[row * 4 + c]
 
+    def to_owners():
+        for kind, t, side in GROUPS:
+            owned[owner_row(kind, t, side):owner_row(kind, t, side) + 4] = natural[
+                stream_row(kind, t, side):stream_row(kind, t, side) + 4
+            ]
+
+    def to_streams():
+        for kind, t, side in GROUPS:
+            natural[stream_row(kind, t, side):stream_row(kind, t, side) + 4] = owned[
+                owner_row(kind, t, side):owner_row(kind, t, side) + 4
+            ]
+
+    for s in range(4):
+        natural[s * 128:(s + 1) * 128] = weight_ref[:, s * 128:(s + 1) * 128].astype(F32).T
+    to_owners()
+    wt_ref[...] = owned[...].astype(BF16)
+    for s in range(4):
+        wb_ref[:, s * 128:(s + 1) * 128] = owned[s * 128:(s + 1) * 128].T.astype(BF16)
+    for s in range(4):
+        natural[s * 128:(s + 1) * 128] = jnp.broadcast_to(biases_ref[s:s + 1], (128, 128)).T
+    to_owners()
+    for half in range(2):
+        lanes = slice(half * 128, (half + 1) * 128)
+        bias_ref[:, lanes] = owned[...]
+        gain_ref[:, lanes] = jnp.broadcast_to(norm_ref[0:1], (128, 128)).T
+        shift_ref[:, lanes] = jnp.broadcast_to(norm_ref[1:2], (128, 128)).T
+
     for c in range(4):
         for b in range(8):
             left[c, b * 128 + 112:(b + 1) * 128] = jnp.zeros((16, 128), BF16)
         for b in range(4):
             right[c, b * 256 + COLS:(b + 1) * 256] = jnp.zeros((16, 128), BF16)
-    dw_ref[...] = jnp.zeros_like(dw_ref)
+    acc[...] = jnp.zeros_like(acc)
+    small[...] = jnp.zeros_like(small)
     acc_gain[...] = jnp.zeros_like(acc_gain)
     acc_shift[...] = jnp.zeros_like(acc_shift)
 
@@ -161,7 +201,6 @@
         )
 
     WHOLE, LOW, HIGH = pl.ds(0, 1024), pl.ds(0, 512), pl.ds(512, 512)
-    far = (col + 2) % 4
 
     def x_send(c):
         def one(source, carry):
@@ -233,8 +272,8 @@
         gate_grad = value_grad * linear[256:512] * (1.0 - gate)
         linear_grad = jnp.concatenate([gate_grad.astype(BF16), value_grad.astype(BF16)], axis=0)
         normed_grad = jnp.dot(wb_ref[...], linear_grad, preferred_element_type=F32)
-        dw_ref[...] += lax.dot_general(
-            linear_grad, normed_s[slot], (((1,), (1,)), ((), ())), preferred_element_type=F32
+        acc[...] += lax.dot_general(
+            normed_s[slot], linear_grad, (((1,), (1,)), ((), ())), preferred_element_type=F32
         )
         scaled = scaled_s[slot]
         acc_gain[...] += normed_grad * scaled
@@ -275,9 +314,79 @@
     for kh in range(2):
         others(lambda there: arrival(send2, recv2, s2, r2, kh, there).wait_recv())
         lax.fori_loop(0, PAIRS, functools.partial(backward, kh), 0)
-    gs_ref[0] = jnp.sum(acc_gain[...].T, axis=0, keepdims=True)
-    gs_ref[1] = jnp.sum(acc_shift[...].T, axis=0, keepdims=True)
-
+
+    for s in range(4):
+        small[s:s + 1] = acc[128:129, s * 128:(s + 1) * 128]
+    small[4:5] = jnp.sum(acc_gain[...].T, axis=0, keepdims=True)
+    small[5:6] = jnp.sum(acc_shift[...].T, axis=0, keepdims=True)
+    for o in range(OWNERS):
+        rows, lane = slice((o // 2) * 8, (o // 2) * 8 + 8), (o % 2) * 256
+        part_s[o, 0:8] = acc[rows, lane:lane + 128]
+        part_s[o, 8:16] = acc[rows, lane + 128:lane + 256]
+        part_s[o, 16:24] = small[...]
+    for r, g in partners:
+        there = r * 4 + g
+        pltpu.make_async_remote_copy(
+            src_ref=part_s.at[there], dst_ref=part_r.at[me], send_sem=as_.at[there], recv_sem=ar.at[me],
+            device_id=(r, col, g), device_id_type=MESH,
+        ).start()
+    part_r[me] = part_s[me]
+
+    def part_arrival(there):
+        return pltpu.make_async_remote_copy(
+            src_ref=part_s.at[there], dst_ref=part_r.at[there], send_sem=as_.at[there], recv_sem=ar.at[there],
+            device_id=(row, col, ch), device_id_type=MESH,
+        )
+
+    others(lambda there: part_arrival(there).wait_recv())
+    total = part_r[0]
+    for o in range(1, OWNERS):
+        total = total + part_r[o]
+    line[col] = total
+
+    def line_copy(slot, there):
+        return pltpu.make_async_remote_copy(
+            src_ref=line.at[slot], dst_ref=line.at[slot], send_sem=bs.at[there], recv_sem=br.at[slot],
+            device_id=(row, there, ch), device_id_type=MESH,
+        )
+
+    for there in (far, east, west):
+        line_copy(col, there).start()
+    for there in (far, east, west):
+        line_copy(there, there).wait_recv()
+    total = (line[0] + line[1]) + (line[2] + line[3])
+    total = total * (1.0 / CROP)
+    whole[me] = total[0:16]
+    small_ref[...] = total[16:24]
+
+    def whole_copy(slot, there, r, g):
+        return pltpu.make_async_remote_copy(
+            src_ref=whole.at[slot], dst_ref=whole.at[slot], send_sem=gs_.at[there], recv_sem=gr.at[slot],
+            device_id=(r, col, g), device_id_type=MESH,
+        )
+
+    for r, g in partners:
+        whole_copy(me, r * 4 + g, r, g).start()
+    others(lambda there: whole_copy(there, there, row, ch).wait_recv())
+    for o in range(OWNERS):
+        rows, lane = slice((o // 2) * 8, (o // 2) * 8 + 8), (o % 2) * 256
+        acc[rows, lane:lane + 128] = whole[o, 0:8]
+        acc[rows, lane + 128:lane + 256] = whole[o, 8:16]
+    for s in range(4):
+        owned[s * 128:(s + 1) * 128] = acc[0:128, s * 128:(s + 1) * 128].T
+    to_streams()
+    for s in range(4):
+        dw_ref[:, s * 128:(s + 1) * 128] = natural[s * 128:(s + 1) * 128].T
+    for s in range(4):
+        owned[s * 128:(s + 1) * 128] = jnp.broadcast_to(small_ref[s:s + 1], (128, 128)).T
+    to_streams()
+    for s in range(4):
+        small_ref[s:s + 1] = natural[s * 128:(s + 1) * 128].T[0:1]
+
+    others(lambda there: part_arrival(there).wait_send())
+    others(lambda there: whole_copy(me, there, row, ch).wait_send())
+    for there in (far, east, west):
+        line_copy(col, there).wait_send()
     for c in range(4):
         def sent(there, carry):
             @pl.when(there != row)
@@ -295,38 +404,17 @@
         others(lambda there: arrival(send2, recv2, s2, r2, kh, there).wait_send())
 
 
-def by_owner(array):
-    lead = array.shape[:-2]
-    n = len(lead)
-    parts = array.reshape(*lead, 2, 2, 4, 8, 4)
-    axes = tuple(range(n)) + tuple(n + a for a in (1, 3, 2, 0, 4))
-    return parts.transpose(axes).reshape(*lead, 512)
-
-
-def by_stream(array):
-    lead = array.shape[:-1]
-    n = len(lead)
-    parts = array.reshape(*lead, 2, 8, 4, 2, 4)
-    axes = tuple(range(n)) + tuple(n + a for a in (3, 0, 2, 1, 4))
-    return parts.transpose(axes).reshape(*lead, 4, 128)
-
-
 def shards(pair, norm_gain, norm_shift, proj_weight, proj_bias, prod_cot):
-    wb = by_owner(proj_weight)
-    wt = wb.T
-    bias = jnp.broadcast_to(by_owner(proj_bias)[:, None], (512, 256))
-    gain = jnp.broadcast_to(norm_gain[:, None], (128, 256))
-    shift = jnp.broadcast_to(norm_shift[:, None], (128, 256))
     vmem = pl.BlockSpec(memory_space=pltpu.VMEM)
     dma = pltpu.SemaphoreType.DMA
-    grad_pair, dw, gs = pl.pallas_call(
+    grad_pair, dw, small = pl.pallas_call(
         kernel,
         out_shape=(
             jax.ShapeDtypeStruct((ROWS, COLS, 128), BF16),
-            jax.ShapeDtypeStruct((512, 144), F32),
-            jax.ShapeDtypeStruct((2, 1, 128), F32),
+            jax.ShapeDtypeStruct((128, 512), F32),
+            jax.ShapeDtypeStruct((8, 128), F32),
         ),
-        in_specs=[vmem] * 7,
+        in_specs=[vmem] * 5,
         out_specs=(vmem,) * 3,
         scratch_shapes=[
             pltpu.VMEM((32, 128, 256), BF16),
@@ -343,21 +431,29 @@
             pltpu.VMEM((2 * PAIRS, 144, 256), BF16),
             pltpu.VMEM((128, 256), F32),
             pltpu.VMEM((128, 256), F32),
+            pltpu.VMEM((512, 128), BF16),
+            pltpu.VMEM((128, 512), BF16),
+            pltpu.VMEM((512, 256), F32),
+            pltpu.VMEM((128, 256), F32),
+            pltpu.VMEM((128, 256), F32),
+            pltpu.VMEM((512, 128), F32),
+            pltpu.VMEM((512, 128), F32),
+            pltpu.VMEM((144, 512), F32),
+            pltpu.VMEM((8, 128), F32),
+            pltpu.VMEM((OWNERS, 24, 128), F32),
+            pltpu.VMEM((OWNERS, 24, 128), F32),
+            pltpu.VMEM((4, 24, 128), F32),
+            pltpu.VMEM((OWNERS, 16, 128), F32),
             dma((4, 8)), dma((4, 8)), dma((4, 2)), dma((4, 2)), dma((4, 2)), dma((4, 2)),
             dma((2, OWNERS)), dma((2, OWNERS)), dma((2, OWNERS)), dma((2, OWNERS)),
+            dma((OWNERS,)), dma((OWNERS,)), dma((4,)), dma((4,)), dma((OWNERS,)), dma((OWNERS,)),
         ],
         compiler_params=pltpu.CompilerParams(
             collective_id=0, has_side_effects=True, vmem_limit_bytes=60 << 20
         ),
         name="triangle_backward",
-    )(pair, prod_cot, wt, wb, bias, gain, shift)
-    sums = jnp.concatenate(
-        [dw[:, 0:128], dw[:, 128].reshape(4, 128), gs.reshape(2, 128)], axis=0
-    )
-    sums = lax.psum(sums, ("row", "col", "ch")) * (1.0 / CROP)
-    grad_weight = by_stream(sums[0:512].T)
-    grad_bias = by_stream(sums[512:516].reshape(512))
-    return grad_pair, grad_weight, grad_bias, sums[516], sums[517]
+    )(pair, prod_cot, proj_weight.reshape(128, 512), proj_bias, jnp.stack([norm_gain, norm_shift]))
+    return grad_pair, dw.reshape(128, 4, 128), small[0:4], small[4], small[5]
 
 
 def solution(mesh):

time: 320 us -> 181 us (0.57)
  waiting for transfers between devices: 143 us -> 0 us
  Pallas kernels: 148 us -> 170 us
  between operations: 14.1 us -> 0.64 us
  local copies, waits for them, and re-layouts: 12.3 us -> 8.68 us
    psum x1 -> x0, waiting for transfers between devices: 143 us -> none  [shards(): sums = lax.psum(sums, ('row', 'col', 'ch')) * (1.0 / CROP)]
    pallas_call x1, Pallas kernels: 148 us -> 170 us  [shards(): pl.pallas_call(kernel, out_shape=(jax.ShapeDtypeStruct((ROWS, COLS, 128),...]
    broadcast_in_dim x4 -> x0, local copies, waits for them, and re-layouts: 3.85 us -> none  [the longest x1 1.39 us: shards(): shift = jnp.broadcast_to(norm_shift[:, None], (128, 256))]
  transfers between devices with their start and end apart: 1 -> 0, of which waited for: 1 -> 0; matrix products, arithmetic and copies ran while one was open for 0% -> 0% of each run, Pallas kernels for 0% -> 0%
where the time goes in v2:
time: 181 us
  Pallas kernels  170 us (94%)
  local copies, waits for them, and re-layouts  8.68 us (5%)
    pallas_call x1, Pallas kernels, shards(): pl.pallas_call(kernel, out_shape=(jax.ShapeDtypeStruct((ROWS, COLS, 128),...  170 us
    unnamed x2, local copies, waits for them, and re-layouts  4.43 us

profile of v2, /device:TPU:1, one launch (start us, length us, event | category | flops | bytes accessed | tf_op | source)
XLA Modules:
  0.0 181.0 jit_solution(4314473043284200593)
XLA Ops:
  0.6 1.6 copy.13
  2.2 1.2 pad_maximum_fusion.norm_ref
  3.5 170.4 %triangle_backward.1 = (bf16[30,240,128]{2,1,0:T(8,128)(2,1)}, f32[128,512]{1,0:T(8,128)}, f32[8,128]{1,0:T(8,128)}) custom-call(bf16[30,240,128]{2,1,0:T(8,128)(2,1)} %pair_ref.1, bf16[32,120,240]{2,1,0:T(8,128)(2,1)} %cot_ref.1, bf16[128,512]{1,0:T(8,128)(2,1)} %bitcast.10, f32[4,128]{1,0:T(4,128)} %biases_ref.1, f32[2,128]{1,0:T(2,128)} %pad_maximum_fusion.norm_ref), custom_call_target="tpu_custom_call" | custom-call | tf_op jit(solution)/shard_map/triangle_backward/pallas_call | solution.py:410
  173.9 1.3 slice_bitcast_fusion
  175.1 1.3 slice.9
  176.4 1.7 reshape.17
  178.1 2.9 %copy.15 = bf16[30,240,128]{2,1,0:T(8,128)(2,1)} copy(bf16[30,240,128]{2,1,0:T(8,128)(2,1)} %get-tuple-element.18) | data formatting | bytes 3686400

commit v3 on v2

--- a/solution.py
+++ b/solution.py
@@ -31,6 +31,8 @@
 OFFSETS.append((0, 0, 1))
 
 
+BACK_CHUNKS = ((0, 0, PAIRS), (1, 0, 8), (1, 8, PAIRS))
+BACK = ((0,), (1, 2))
 GROUPS = [(kind, t, side) for kind in range(2) for t in range(OWNERS) for side in range(2)]
 
 
@@ -43,7 +45,7 @@
 
 
 def kernel(
-    pair_ref, cot_ref, weight_ref, biases_ref, norm_ref,
+    pair_ref, cot_ref, weight_ref, biases_ref, gains_ref, shifts_ref,
     grad_ref, dw_ref, small_ref,
     stage, cotf, send1, recv1, left, right, wide, send2, recv2, scaled_s, inv_s, normed_s, acc_gain, acc_shift,
     wt_ref, wb_ref, bias_ref, gain_ref, shift_ref, natural, owned, acc, small, part_s, part_r, line, whole,
@@ -67,35 +69,70 @@
     for c in (east, west, far):
         pl.semaphore_signal(barrier, 1, device_id=(row, c, ch), device_id_type=MESH)
 
-    def stage_one(c, carry):
-        stage[c] = jnp.zeros((128, 256), BF16)
-        stage[c, 0:120, 0:COLS] = cot_ref[c]
+    def stage_one(pair, carry):
+        stage[pair] = jnp.zeros((240, 256), BF16)
+        stage[pair, 0:120, 0:COLS] = cot_ref[2 * pair]
+        stage[pair, 120:240, 0:COLS] = cot_ref[2 * pair + 1]
         return carry
 
-    lax.fori_loop(0, 32, stage_one, 0)
+    lax.fori_loop(0, 16, stage_one, 0)
     pl.semaphore_wait(barrier, len(partners) + 3)
 
-    def cot_copy(c, there):
-        return pltpu.make_async_remote_copy(
-            src_ref=stage.at[there * 4 + c],
-            dst_ref=cotf.at[c, col, pl.ds(row * 128, 128)],
-            send_sem=cs.at[c, there], recv_sem=cr.at[c, row],
+    def cot_copy(there):
+        return pltpu.make_async_remote_copy(
+            src_ref=stage.at[pl.ds(there * 2, 2)], dst_ref=cotf.at[col, row],
+            send_sem=cs.at[there], recv_sem=cr.at[row],
             device_id=(there, col, ch), device_id_type=MESH,
         )
 
-    def cot_arrival(c, source):
-        return pltpu.make_async_remote_copy(
-            src_ref=stage.at[c],
-            dst_ref=cotf.at[c, col, pl.ds(source * 128, 128)],
-            send_sem=cs.at[c, source], recv_sem=cr.at[c, source],
+    def cot_arrival(source):
+        return pltpu.make_async_remote_copy(
+            src_ref=stage.at[pl.ds(source * 2, 2)], dst_ref=cotf.at[col, source],
+            send_sem=cs.at[source], recv_sem=cr.at[source],
             device_id=(row, col, ch), device_id_type=MESH,
         )
 
-    for c in range(4):
-        for step in (6, 5, 7, 2, 4, 1, 3):
-            there = ((row // 4 + step // 4) % 2) * 4 + (row + step) % 4
-            cot_copy(c, there).start()
-        cotf[c, col, pl.ds(row * 128, 128)] = stage[row * 4 + c]
+    def x_copy(block, r, sems, recvs, side, there):
+        return pltpu.make_async_remote_copy(
+            src_ref=cotf.at[block, r], dst_ref=cotf.at[block, r],
+            send_sem=sems.at[r, side], recv_sem=recvs.at[r, side],
+            device_id=(row, there, ch), device_id_type=MESH,
+        )
+
+    def x_relay(block, r, side, there):
+        return pltpu.make_async_remote_copy(
+            src_ref=cotf.at[block, r, side], dst_ref=cotf.at[block, r, side],
+            send_sem=fs.at[r, side], recv_sem=fr.at[r, side],
+            device_id=(row, there, ch), device_id_type=MESH,
+        )
+
+    blocks = [row]
+    for step in (6, 5, 7, 2, 4, 1, 3):
+        z_lo = (row // 4 + step // 4) % 2
+        cot_copy(z_lo * 4 + (row + step) % 4).start()
+        blocks.append(z_lo * 4 + (row + 8 - step) % 4)
+    cotf[col, row] = stage[pl.ds(row * 2, 2)]
+
+    def x_send(n):
+        r = blocks[n]
+        if n > 0:
+            cot_arrival(r).wait_recv()
+        x_copy(col, r, xs, xr, 0, east).start()
+        x_copy(col, r, xs, xr, 1, west).start()
+
+    def x_forward(n):
+        r = blocks[n]
+        x_copy(west, r, xs, xr, 0, east).wait_recv()
+        x_relay(west, r, 0, east).start()
+        x_copy(east, r, xs, xr, 1, west).wait_recv()
+        x_relay(east, r, 1, west).start()
+
+    def x_finish(n):
+        r = blocks[n]
+        x_relay(far, r, 0, east).wait_recv()
+        x_relay(far, r, 1, west).wait_recv()
+
+    x_send(0)
 
     def to_owners():
         for kind, t, side in GROUPS:
@@ -121,14 +158,13 @@
     for half in range(2):
         lanes = slice(half * 128, (half + 1) * 128)
         bias_ref[:, lanes] = owned[...]
-        gain_ref[:, lanes] = jnp.broadcast_to(norm_ref[0:1], (128, 128)).T
-        shift_ref[:, lanes] = jnp.broadcast_to(norm_ref[1:2], (128, 128)).T
-
-    for c in range(4):
-        for b in range(8):
-            left[c, b * 128 + 112:(b + 1) * 128] = jnp.zeros((16, 128), BF16)
-        for b in range(4):
-            right[c, b * 256 + COLS:(b + 1) * 256] = jnp.zeros((16, 128), BF16)
+        gain_ref[:, lanes] = jnp.broadcast_to(gains_ref[...], (128, 128)).T
+        shift_ref[:, lanes] = jnp.broadcast_to(shifts_ref[...], (128, 128)).T
+
+    left[...] = jnp.zeros_like(left)
+    for p in range(2):
+        for x in range(4):
+            right[p, x, COLS:256] = jnp.zeros((16, 256), BF16)
     acc[...] = jnp.zeros_like(acc)
     small[...] = jnp.zeros_like(small)
     acc_gain[...] = jnp.zeros_like(acc_gain)
@@ -193,36 +229,6 @@
 
         lax.fori_loop(0, OWNERS, one, 0)
 
-    def x_copy(c, block, part, sems, recvs, side, there):
-        return pltpu.make_async_remote_copy(
-            src_ref=cotf.at[c, block, part], dst_ref=cotf.at[c, block, part],
-            send_sem=sems.at[c, side], recv_sem=recvs.at[c, side],
-            device_id=(row, there, ch), device_id_type=MESH,
-        )
-
-    WHOLE, LOW, HIGH = pl.ds(0, 1024), pl.ds(0, 512), pl.ds(512, 512)
-
-    def x_send(c):
-        def one(source, carry):
-            @pl.when(source != row)
-            def _():
-                cot_arrival(c, source).wait_recv()
-            return carry
-
-        lax.fori_loop(0, 8, one, 0)
-        x_copy(c, col, WHOLE, xs, xr, 0, east).start()
-        x_copy(c, col, WHOLE, xs, xr, 1, west).start()
-
-    def x_forward(c):
-        x_copy(c, west, WHOLE, xs, xr, 0, east).wait_recv()
-        x_copy(c, west, LOW, fs, fr, 0, east).start()
-        x_copy(c, east, WHOLE, xs, xr, 1, west).wait_recv()
-        x_copy(c, east, HIGH, fs, fr, 1, west).start()
-
-    def x_finish(c):
-        x_copy(c, far, LOW, fs, fr, 0, east).wait_recv()
-        x_copy(c, far, HIGH, fs, fr, 1, west).wait_recv()
-
     def regroup(kh):
         others(lambda there: arrival(send1, recv1, s1, r1, kh, there).wait_recv())
 
@@ -231,24 +237,42 @@
             return carry
 
         lax.fori_loop(0, OWNERS, widen, 0)
-        for c in range(4):
-            for b in range(8):
-                left[c, b * 128:b * 128 + 120] = wide[pl.ds(b * 960 + c, 120, stride=8)].astype(BF16)
-            for b in range(4):
-                right[c, b * 256:b * 256 + COLS] = wide[pl.ds(b * 1920 + 4 + c, COLS, stride=8)].astype(BF16)
-
-    def triangle(c):
-        for b in range(8):
-            rows = pl.ds(b * 128, 128)
-            total = jnp.zeros((128, 128), F32)
+        for p in range(2):
+            for q in range(2):
+                lanes = slice(q * 128, q * 128 + 128)
+                for r in range(8):
+                    left[p, r, q * 120:q * 120 + 120, lanes] = wide[
+                        pl.ds(r * 960 + 2 * p + q, 120, stride=8)
+                    ].astype(BF16)
+                for x in range(4):
+                    right[p, x, 0:COLS, lanes] = wide[
+                        pl.ds(x * 1920 + 4 + 2 * p + q, COLS, stride=8)
+                    ].astype(BF16)
+
+    def triangle(group, first):
+        for n in group:
+            r = blocks[n]
+            for p in range(2):
+                total = jnp.dot(cotf[0, r, p], right[p, 0], preferred_element_type=F32)
+                for x in range(1, 4):
+                    total += jnp.dot(cotf[x, r, p], right[p, x], preferred_element_type=F32)
+                for q in range(2):
+                    wide[pl.ds(r * 960 + 2 * p + q, 120, stride=8)] = total[
+                        q * 120:q * 120 + 120, q * 128:q * 128 + 128
+                    ]
+        for p in range(2):
             for x in range(4):
-                total += jnp.dot(cotf[c, x, rows], right[c, x * 256:(x + 1) * 256], preferred_element_type=F32)
-            wide[pl.ds(b * 960 + c, 120, stride=8)] = total[0:120]
-        for x in range(4):
-            total = lax.dot_general(
-                cotf[c, x], left[c], (((0,), (0,)), ((), ())), preferred_element_type=F32
-            )
-            wide[pl.ds(x * 1920 + 4 + c, COLS, stride=8)] = total[0:COLS]
+                total = None
+                for n in group:
+                    term = lax.dot_general(
+                        cotf[x, blocks[n], p], left[p, blocks[n]], (((0,), (0,)), ((), ())),
+                        preferred_element_type=F32,
+                    )
+                    total = term if total is None else total + term
+                for q in range(2):
+                    rows = pl.ds(x * 1920 + 4 + 2 * p + q, COLS, stride=8)
+                    part = total[0:COLS, q * 128:q * 128 + 128]
+                    wide[rows] = part if first else wide[rows] + part
 
     def give_back(kh):
         def narrow(target, carry):
@@ -256,7 +280,19 @@
             return carry
 
         lax.fori_loop(0, OWNERS, narrow, 0)
-        send_all(send2, recv2, s2, r2, kh)
+        for n in BACK[kh]:
+            for r, g in partners:
+                back_copy(n, r * 4 + g, me, r, g).start()
+        recv2[kh, me] = send2[kh, me]
+
+    def back_copy(n, source, target, r, g):
+        kh, start, stop = BACK_CHUNKS[n]
+        rows = pl.ds(start * 16, (stop - start) * 16)
+        return pltpu.make_async_remote_copy(
+            src_ref=send2.at[kh, source, rows], dst_ref=recv2.at[kh, target, rows],
+            send_sem=s2.at[n, source], recv_sem=r2.at[n, target],
+            device_id=(r, col, g), device_id_type=MESH,
+        )
 
     def backward(kh, ip, carry):
         width = HALF_COLS[kh]
@@ -287,33 +323,42 @@
             grad_ref[2 * ip + half, kh * 128:kh * 128 + width] = out[0:width]
         return carry
 
-    lax.fori_loop(0, PAIRS, functools.partial(forward, 0), 0)
+    lax.fori_loop(0, 8, functools.partial(forward, 0), 0)
+    x_send(1)
+    lax.fori_loop(8, PAIRS, functools.partial(forward, 0), 0)
     send_all(send1, recv1, s1, r1, 0)
-    x_send(0)
-    lax.fori_loop(0, 8, functools.partial(forward, 1), 0)
-    x_send(1)
-    lax.fori_loop(8, PAIRS, functools.partial(forward, 1), 0)
-    send_all(send1, recv1, s1, r1, 1)
     x_send(2)
     x_forward(0)
+    lax.fori_loop(0, 5, functools.partial(forward, 1), 0)
     x_send(3)
     x_forward(1)
+    lax.fori_loop(5, 10, functools.partial(forward, 1), 0)
+    x_send(4)
+    x_forward(2)
+    lax.fori_loop(10, PAIRS, functools.partial(forward, 1), 0)
+    send_all(send1, recv1, s1, r1, 1)
+    x_send(5)
+    x_forward(3)
+    x_send(6)
+    x_forward(4)
+    x_send(7)
+    x_forward(5)
     regroup(0)
-    x_forward(2)
-    x_finish(0)
-    triangle(0)
-    x_forward(3)
-    for c in range(1, 4):
-        x_finish(c)
-        triangle(c)
+    x_forward(6)
+    for n in range(6):
+        x_finish(n)
+    triangle(range(0, 6), True)
+    x_forward(7)
+    x_finish(6)
+    x_finish(7)
+    triangle(range(6, 8), False)
     give_back(0)
     regroup(1)
-    for c in range(4):
-        triangle(c)
+    triangle(range(0, 8), True)
     give_back(1)
-    for kh in range(2):
-        others(lambda there: arrival(send2, recv2, s2, r2, kh, there).wait_recv())
-        lax.fori_loop(0, PAIRS, functools.partial(backward, kh), 0)
+    for n, (kh, start, stop) in enumerate(BACK_CHUNKS):
+        others(lambda there: back_copy(n, there, there, row, ch).wait_recv())
+        lax.fori_loop(start, stop, functools.partial(backward, kh), 0)
 
     for s in range(4):
         small[s:s + 1] = acc[128:129, s * 128:(s + 1) * 128]
@@ -387,21 +432,18 @@
     others(lambda there: whole_copy(me, there, row, ch).wait_send())
     for there in (far, east, west):
         line_copy(col, there).wait_send()
-    for c in range(4):
-        def sent(there, carry):
-            @pl.when(there != row)
-            def _():
-                cot_copy(c, there).wait_send()
-            return carry
-
-        lax.fori_loop(0, 8, sent, 0)
-        x_copy(c, col, WHOLE, xs, xr, 0, east).wait_send()
-        x_copy(c, col, WHOLE, xs, xr, 1, west).wait_send()
-        x_copy(c, west, LOW, fs, fr, 0, east).wait_send()
-        x_copy(c, east, HIGH, fs, fr, 1, west).wait_send()
+    for n in range(8):
+        r = blocks[n]
+        if n > 0:
+            cot_copy(r).wait_send()
+        x_copy(col, r, xs, xr, 0, east).wait_send()
+        x_copy(col, r, xs, xr, 1, west).wait_send()
+        x_relay(west, r, 0, east).wait_send()
+        x_relay(east, r, 1, west).wait_send()
     for kh in range(2):
         others(lambda there: arrival(send1, recv1, s1, r1, kh, there).wait_send())
-        others(lambda there: arrival(send2, recv2, s2, r2, kh, there).wait_send())
+    for n in range(len(BACK_CHUNKS)):
+        others(lambda there: back_copy(n, there, there, row, ch).wait_send())
 
 
 def shards(pair, norm_gain, norm_shift, proj_weight, proj_bias, prod_cot):
@@ -414,15 +456,15 @@
             jax.ShapeDtypeStruct((128, 512), F32),
             jax.ShapeDtypeStruct((8, 128), F32),
         ),
-        in_specs=[vmem] * 5,
+        in_specs=[vmem] * 6,
         out_specs=(vmem,) * 3,
         scratch_shapes=[
-            pltpu.VMEM((32, 128, 256), BF16),
-            pltpu.VMEM((4, 4, 1024, 256), BF16),
+            pltpu.VMEM((16, 240, 256), BF16),
+            pltpu.VMEM((4, 8, 2, 240, 256), BF16),
             pltpu.VMEM((2, OWNERS, 240, 128), BF16),
             pltpu.VMEM((2, OWNERS, 240, 128), BF16),
-            pltpu.VMEM((4, 1024, 128), BF16),
-            pltpu.VMEM((4, 1024, 128), BF16),
+            pltpu.VMEM((2, 8, 240, 256), BF16),
+            pltpu.VMEM((2, 4, 256, 256), BF16),
             pltpu.VMEM((CROP * 8, 128), F32),
             pltpu.VMEM((2, OWNERS, 240, 128), BF16),
             pltpu.VMEM((2, OWNERS, 240, 128), BF16),
@@ -444,15 +486,15 @@
             pltpu.VMEM((OWNERS, 24, 128), F32),
             pltpu.VMEM((4, 24, 128), F32),
             pltpu.VMEM((OWNERS, 16, 128), F32),
-            dma((4, 8)), dma((4, 8)), dma((4, 2)), dma((4, 2)), dma((4, 2)), dma((4, 2)),
-            dma((2, OWNERS)), dma((2, OWNERS)), dma((2, OWNERS)), dma((2, OWNERS)),
+            dma((8,)), dma((8,)), dma((8, 2)), dma((8, 2)), dma((8, 2)), dma((8, 2)),
+            dma((2, OWNERS)), dma((2, OWNERS)), dma((3, OWNERS)), dma((3, OWNERS)),
             dma((OWNERS,)), dma((OWNERS,)), dma((4,)), dma((4,)), dma((OWNERS,)), dma((OWNERS,)),
         ],
         compiler_params=pltpu.CompilerParams(
             collective_id=0, has_side_effects=True, vmem_limit_bytes=60 << 20
         ),
         name="triangle_backward",
-    )(pair, prod_cot, proj_weight.reshape(128, 512), proj_bias, jnp.stack([norm_gain, norm_shift]))
+    )(pair, prod_cot, proj_weight.reshape(128, 512), proj_bias, norm_gain.reshape(1, 128), norm_shift.reshape(1, 128))
     return grad_pair, dw.reshape(128, 4, 128), small[0:4], small[4], small[5]
 
 

time: 181 us -> 173 us (0.956)
  Pallas kernels: 170 us -> 163 us
    pallas_call x1, Pallas kernels: 170 us -> 163 us  [shards(): pl.pallas_call(kernel, out_shape=(jax.ShapeDtypeStruct((ROWS, COLS, 128),...]
where the time goes in v3:
time: 173 us; the launch traced here: 172 us
  Pallas kernels  163 us (94%)
  local copies, waits for them, and re-layouts  8.68 us (5%)
    pallas_call x1, Pallas kernels, shards(): pl.pallas_call(kernel, out_shape=(jax.ShapeDtypeStruct((ROWS, COLS, 128),...  163 us
    unnamed x2, local copies, waits for them, and re-layouts  4.43 us

profile of v3, /device:TPU:1, one launch (start us, length us, event | category | flops | bytes accessed | tf_op | source)
XLA Modules:
  0.0 172.3 jit_solution(17066728267626890692)
XLA Ops:
  0.6 1.6 copy.13
  2.2 162.9 %triangle_backward.1 = (bf16[30,240,128]{2,1,0:T(8,128)(2,1)}, f32[128,512]{1,0:T(8,128)}, f32[8,128]{1,0:T(8,128)}) custom-call(bf16[30,240,128]{2,1,0:T(8,128)(2,1)} %pair_ref.1, bf16[32,120,240]{2,1,0:T(8,128)(2,1)} %cot_ref.1, bf16[128,512]{1,0:T(8,128)(2,1)} %bitcast.10, f32[4,128]{1,0:T(4,128)} %biases_ref.1, f32[1,128]{1,0:T(1,128)} %bitcast.12, ...), custom_call_target="tpu_custom_call" | custom-call | tf_op jit(solution)/shard_map/triangle_backward/pallas_call | solution.py:452
  165.1 1.3 slice_bitcast_fusion
  166.4 1.3 slice.9
  167.7 1.7 %reshape.25 = f32[128,4,128]{2,1,0:T(4,128)} reshape(f32[128,512]{1,0:T(8,128)} %get-tuple-element.9) | data formatting | bytes 524288 | tf_op jit(solution)/shard_map/reshape | solution.py:498
  169.4 2.9 %copy.15 = bf16[30,240,128]{2,1,0:T(8,128)(2,1)} copy(bf16[30,240,128]{2,1,0:T(8,128)(2,1)} %get-tuple-element.18) | data formatting | bytes 3686400

commit v4 on v3

--- a/solution.py
+++ b/solution.py
@@ -24,11 +24,7 @@
     (2, 0), (0, 2),
     (1, 0), (0, 1), (3, 0), (0, 3),
 )
-OFFSETS = []
-for start in range(0, len(STEPS), 1):
-    OFFSETS.append((*STEPS[start], 0))
-    OFFSETS.append((*STEPS[start], 1))
-OFFSETS.append((0, 0, 1))
+OFFSETS = [(dz, dy, core) for core in range(2) for dz, dy in STEPS] + [(0, 0, 1)]
 
 
 BACK_CHUNKS = ((0, 0, PAIRS), (1, 0, 8), (1, 8, PAIRS))
@@ -146,8 +142,9 @@
                 owner_row(kind, t, side):owner_row(kind, t, side) + 4
             ]
 
-    for s in range(4):
-        natural[s * 128:(s + 1) * 128] = weight_ref[:, s * 128:(s + 1) * 128].astype(F32).T
+    weights = weight_ref[...].astype(F32)
+    for s in range(4):
+        natural[s * 128:(s + 1) * 128] = weights[:, s, :].T
     to_owners()
     wt_ref[...] = owned[...].astype(BF16)
     for s in range(4):
@@ -364,11 +361,15 @@
         small[s:s + 1] = acc[128:129, s * 128:(s + 1) * 128]
     small[4:5] = jnp.sum(acc_gain[...].T, axis=0, keepdims=True)
     small[5:6] = jnp.sum(acc_shift[...].T, axis=0, keepdims=True)
+    coarse = small[...].astype(BF16)
+    fine = small[...] - coarse.astype(F32)
+    small_parts = jnp.concatenate([coarse.astype(F32), fine], axis=0).astype(BF16)
     for o in range(OWNERS):
         rows, lane = slice((o // 2) * 8, (o // 2) * 8 + 8), (o % 2) * 256
-        part_s[o, 0:8] = acc[rows, lane:lane + 128]
-        part_s[o, 8:16] = acc[rows, lane + 128:lane + 256]
-        part_s[o, 16:24] = small[...]
+        part_s[o, 0:16] = jnp.concatenate(
+            [acc[rows, lane:lane + 128], acc[rows, lane + 128:lane + 256]], axis=0
+        ).astype(BF16)
+        part_s[o, 16:32] = small_parts
     for r, g in partners:
         there = r * 4 + g
         pltpu.make_async_remote_copy(
@@ -384,10 +385,11 @@
         )
 
     others(lambda there: part_arrival(there).wait_recv())
-    total = part_r[0]
+    total = part_r[0].astype(F32)
     for o in range(1, OWNERS):
-        total = total + part_r[o]
-    line[col] = total
+        total = total + part_r[o].astype(F32)
+    line[col, 0:16] = total[0:16]
+    line[col, 16:24] = total[16:24] + total[24:32]
 
     def line_copy(slot, there):
         return pltpu.make_async_remote_copy(
@@ -421,7 +423,7 @@
         owned[s * 128:(s + 1) * 128] = acc[0:128, s * 128:(s + 1) * 128].T
     to_streams()
     for s in range(4):
-        dw_ref[:, s * 128:(s + 1) * 128] = natural[s * 128:(s + 1) * 128].T
+        dw_ref[:, s, :] = natural[s * 128:(s + 1) * 128].T
     for s in range(4):
         owned[s * 128:(s + 1) * 128] = jnp.broadcast_to(small_ref[s:s + 1], (128, 128)).T
     to_streams()
@@ -453,7 +455,7 @@
         kernel,
         out_shape=(
             jax.ShapeDtypeStruct((ROWS, COLS, 128), BF16),
-            jax.ShapeDtypeStruct((128, 512), F32),
+            jax.ShapeDtypeStruct((128, 4, 128), F32),
             jax.ShapeDtypeStruct((8, 128), F32),
         ),
         in_specs=[vmem] * 6,
@@ -482,8 +484,8 @@
             pltpu.VMEM((512, 128), F32),
             pltpu.VMEM((144, 512), F32),
             pltpu.VMEM((8, 128), F32),
-            pltpu.VMEM((OWNERS, 24, 128), F32),
-            pltpu.VMEM((OWNERS, 24, 128), F32),
+            pltpu.VMEM((OWNERS, 32, 128), BF16),
+            pltpu.VMEM((OWNERS, 32, 128), BF16),
             pltpu.VMEM((4, 24, 128), F32),
             pltpu.VMEM((OWNERS, 16, 128), F32),
             dma((8,)), dma((8,)), dma((8, 2)), dma((8, 2)), dma((8, 2)), dma((8, 2)),
@@ -494,8 +496,8 @@
             collective_id=0, has_side_effects=True, vmem_limit_bytes=60 << 20
         ),
         name="triangle_backward",
-    )(pair, prod_cot, proj_weight.reshape(128, 512), proj_bias, norm_gain.reshape(1, 128), norm_shift.reshape(1, 128))
-    return grad_pair, dw.reshape(128, 4, 128), small[0:4], small[4], small[5]
+    )(pair, prod_cot, proj_weight, proj_bias, norm_gain.reshape(1, 128), norm_shift.reshape(1, 128))
+    return grad_pair, dw, small[0:4], small[4], small[5]
 
 
 def solution(mesh):

time: 173 us -> 166 us (0.960)
  Pallas kernels: 163 us -> 159 us
  local copies, waits for them, and re-layouts: 8.68 us -> 6.14 us
    pallas_call x1, Pallas kernels: 163 us -> 159 us  [shards(): pl.pallas_call(kernel, out_shape=(jax.ShapeDtypeStruct((ROWS, COLS, 128),...]
    reshape x1 -> x0, local copies, waits for them, and re-layouts: 1.74 us -> none  [shards(): return (grad_pair, dw.reshape(128, 4, 128), small[0:4], small[4], small[5])]
    unnamed x2 -> x4, local copies, waits for them, and re-layouts: 4.43 us -> 3.6 us
where the time goes in v4:
time: 166 us; the launch traced here: 165 us
  Pallas kernels  159 us (96%)
  local copies, waits for them, and re-layouts  6.14 us (4%)
    pallas_call x1, Pallas kernels, shards(): pl.pallas_call(kernel, out_shape=(jax.ShapeDtypeStruct((ROWS, COLS, 128),...  159 us
    unnamed x4, local copies, waits for them, and re-layouts  3.6 us

profile of v4, /device:TPU:1, one launch (start us, length us, event | category | flops | bytes accessed | tf_op | source)
XLA Modules:
  0.0 165.4 jit_solution(5666218240726468264)
XLA Ops:
  0.6 158.6 %triangle_backward.1 = (bf16[30,240,128]{2,1,0:T(8,128)(2,1)}, f32[128,4,128]{2,1,0:T(4,128)}, f32[8,128]{1,0:T(8,128)}) custom-call(bf16[30,240,128]{2,1,0:T(8,128)(2,1)} %pair_ref.1, bf16[32,120,240]{2,1,0:T(8,128)(2,1)} %cot_ref.1, bf16[128,4,128]{2,1,0:T(4,128)(2,1)} %weight_ref.1, f32[4,128]{1,0:T(4,128)} %biases_ref.1, f32[1,128]{1,0:T(1,128)} %bitcast.6, ...), custom_call_target="tpu_custom_call" | custom-call | tf_op jit(solution)/shard_map/triangle_backward/pallas_call | solution.py:454
  159.2 1.3 slice_bitcast_fusion
  160.5 1.3 slice.9
  161.8 0.0 copy-start
  161.8 2.9 %copy.13 = bf16[30,240,128]{2,1,0:T(8,128)(2,1)} copy(bf16[30,240,128]{2,1,0:T(8,128)(2,1)} %get-tuple-element.18) | data formatting | bytes 3686400
  164.7 0.0 copy-done
  164.7 0.7 copy.14
Async XLA Ops:
  161.8 2.9 %copy-start = (f32[128,4,128]{2,1,0:T(4,128)S(1)}, f32[128,4,128]{2,1,0:T(4,128)}, u32[]{:S(2)}) copy-start(f32[128,4,128]{2,1,0:T(4,128)} %get-tuple-element.19) | copy-start | bytes 786436

commit v5 on v4

--- a/solution.py
+++ b/solution.py
@@ -27,7 +27,8 @@
 OFFSETS = [(dz, dy, core) for core in range(2) for dz, dy in STEPS] + [(0, 0, 1)]
 
 
-BACK_CHUNKS = ((0, 0, PAIRS), (1, 0, 8), (1, 8, PAIRS))
+LAST = 8
+BACK_CHUNKS = ((0, 0, PAIRS), (1, 0, LAST), (1, LAST, PAIRS))
 BACK = ((0,), (1, 2))
 GROUPS = [(kind, t, side) for kind in range(2) for t in range(OWNERS) for side in range(2)]
 
@@ -41,10 +42,11 @@
 
 
 def kernel(
-    pair_ref, cot_ref, weight_ref, biases_ref, gains_ref, shifts_ref,
-    grad_ref, dw_ref, small_ref,
+    pair_hbm, cot_ref, weight_ref, biases_ref, gains_ref, shifts_ref,
+    grad_hbm, dw_ref, bias_out, gain_out, shift_out,
     stage, cotf, send1, recv1, left, right, wide, send2, recv2, scaled_s, inv_s, normed_s, acc_gain, acc_shift,
     wt_ref, wb_ref, bias_ref, gain_ref, shift_ref, natural, owned, acc, small, part_s, part_r, line, whole,
+    pair_ref, grad_ref, late, io,
     cs, cr, xs, xr, fs, fr, s1, r1, s2, r2, as_, ar, bs, br, gs_, gr,
 ):
     row, col, ch = lax.axis_index("row"), lax.axis_index("col"), lax.axis_index("ch")
@@ -59,6 +61,8 @@
         z2, y2, k2 = (z + dz) % 4, (y + dy) % 4, (core + dk) % 2
         partners.append(((z2 % 2) * 4 + y2, (z2 // 2) * 2 + k2))
 
+    load = pltpu.make_async_copy(pair_hbm, pair_ref, io.at[0])
+    load.start()
     barrier = pltpu.get_barrier_semaphore()
     for r, g in partners:
         pl.semaphore_signal(barrier, 1, device_id=(r, col, g), device_id_type=MESH)
@@ -291,8 +295,7 @@
             device_id=(r, col, g), device_id_type=MESH,
         )
 
-    def backward(kh, ip, carry):
-        width = HALF_COLS[kh]
+    def backward(kh, deferred, ip, carry):
         slot = kh * PAIRS + ip
         back = recv2[kh, :, pl.ds(pl.multiple_of(ip * 16, 16), 16), :].astype(F32)
         side_grad = jnp.concatenate(
@@ -308,9 +311,18 @@
         acc[...] += lax.dot_general(
             normed_s[slot], linear_grad, (((1,), (1,)), ((), ())), preferred_element_type=F32
         )
+        acc_gain[...] += normed_grad * scaled_s[slot]
+        acc_shift[...] += normed_grad
+        if deferred:
+            late[ip - LAST] = normed_grad
+        else:
+            pair_gradient(kh, ip, normed_grad)
+        return carry
+
+    def pair_gradient(kh, ip, normed_grad):
+        width = HALF_COLS[kh]
+        slot = kh * PAIRS + ip
         scaled = scaled_s[slot]
-        acc_gain[...] += normed_grad * scaled
-        acc_shift[...] += normed_grad
         gained = normed_grad * gain_ref[...]
         centre = jnp.mean(gained, axis=0, keepdims=True)
         slope = jnp.mean(gained * scaled, axis=0, keepdims=True)
@@ -318,8 +330,12 @@
         for half in range(2):
             out = result[:, half * 128:(half + 1) * 128].T.astype(BF16)
             grad_ref[2 * ip + half, kh * 128:kh * 128 + width] = out[0:width]
+
+    def finish_late(ip, carry):
+        pair_gradient(1, ip, late[ip - LAST])
         return carry
 
+    load.wait()
     lax.fori_loop(0, 8, functools.partial(forward, 0), 0)
     x_send(1)
     lax.fori_loop(8, PAIRS, functools.partial(forward, 0), 0)
@@ -355,7 +371,7 @@
     give_back(1)
     for n, (kh, start, stop) in enumerate(BACK_CHUNKS):
         others(lambda there: back_copy(n, there, there, row, ch).wait_recv())
-        lax.fori_loop(start, stop, functools.partial(backward, kh), 0)
+        lax.fori_loop(start, stop, functools.partial(backward, kh, kh == 1 and start == LAST), 0)
 
     for s in range(4):
         small[s:s + 1] = acc[128:129, s * 128:(s + 1) * 128]
@@ -377,6 +393,9 @@
             device_id=(r, col, g), device_id_type=MESH,
         ).start()
     part_r[me] = part_s[me]
+    lax.fori_loop(LAST, PAIRS, finish_late, 0)
+    store = pltpu.make_async_copy(grad_ref, grad_hbm, io.at[1])
+    store.start()
 
     def part_arrival(there):
         return pltpu.make_async_remote_copy(
@@ -404,7 +423,9 @@
     total = (line[0] + line[1]) + (line[2] + line[3])
     total = total * (1.0 / CROP)
     whole[me] = total[0:16]
-    small_ref[...] = total[16:24]
+    small[...] = total[16:24]
+    gain_out[...] = small[4:5]
+    shift_out[...] = small[5:6]
 
     def whole_copy(slot, there, r, g):
         return pltpu.make_async_remote_copy(
@@ -425,11 +446,12 @@
     for s in range(4):
         dw_ref[:, s, :] = natural[s * 128:(s + 1) * 128].T
     for s in range(4):
-        owned[s * 128:(s + 1) * 128] = jnp.broadcast_to(small_ref[s:s + 1], (128, 128)).T
+        owned[s * 128:(s + 1) * 128] = jnp.broadcast_to(small[s:s + 1], (128, 128)).T
     to_streams()
     for s in range(4):
-        small_ref[s:s + 1] = natural[s * 128:(s + 1) * 128].T[0:1]
-
+        bias_out[s:s + 1] = natural[s * 128:(s + 1) * 128].T[0:1]
+
+    store.wait()
     others(lambda there: part_arrival(there).wait_send())
     others(lambda there: whole_copy(me, there, row, ch).wait_send())
     for there in (far, east, west):
@@ -451,15 +473,17 @@
 def shards(pair, norm_gain, norm_shift, proj_weight, proj_bias, prod_cot):
     vmem = pl.BlockSpec(memory_space=pltpu.VMEM)
     dma = pltpu.SemaphoreType.DMA
-    grad_pair, dw, small = pl.pallas_call(
+    grad_pair, dw, bias, gain, shift = pl.pallas_call(
         kernel,
         out_shape=(
             jax.ShapeDtypeStruct((ROWS, COLS, 128), BF16),
             jax.ShapeDtypeStruct((128, 4, 128), F32),
-            jax.ShapeDtypeStruct((8, 128), F32),
+            jax.ShapeDtypeStruct((4, 128), F32),
+            jax.ShapeDtypeStruct((1, 128), F32),
+            jax.ShapeDtypeStruct((1, 128), F32),
         ),
-        in_specs=[vmem] * 6,
-        out_specs=(vmem,) * 3,
+        in_specs=[pl.BlockSpec(memory_space=pl.ANY)] + [vmem] * 5,
+        out_specs=(pl.BlockSpec(memory_space=pl.ANY),) + (vmem,) * 4,
         scratch_shapes=[
             pltpu.VMEM((16, 240, 256), BF16),
             pltpu.VMEM((4, 8, 2, 240, 256), BF16),
@@ -488,6 +512,10 @@
             pltpu.VMEM((OWNERS, 32, 128), BF16),
             pltpu.VMEM((4, 24, 128), F32),
             pltpu.VMEM((OWNERS, 16, 128), F32),
+            pltpu.VMEM((ROWS, COLS, 128), BF16),
+            pltpu.VMEM((ROWS, COLS, 128), BF16),
+            pltpu.VMEM((PAIRS - LAST, 128, 256), F32),
+            dma((2,)),
             dma((8,)), dma((8,)), dma((8, 2)), dma((8, 2)), dma((8, 2)), dma((8, 2)),
             dma((2, OWNERS)), dma((2, OWNERS)), dma((3, OWNERS)), dma((3, OWNERS)),
             dma((OWNERS,)), dma((OWNERS,)), dma((4,)), dma((4,)), dma((OWNERS,)), dma((OWNERS,)),
@@ -497,7 +525,7 @@
         ),
         name="triangle_backward",
     )(pair, prod_cot, proj_weight, proj_bias, norm_gain.reshape(1, 128), norm_shift.reshape(1, 128))
-    return grad_pair, dw, small[0:4], small[4], small[5]
+    return grad_pair, dw, bias, gain.reshape(128), shift.reshape(128)
 
 
 def solution(mesh):

time: 166 us -> 163 us (0.982)
  Pallas kernels: 159 us -> 157 us
    unnamed x4 -> x13, local copies, waits for them, and re-layouts: 3.6 us -> 5.21 us
where the time goes in v5:
time: 163 us
  Pallas kernels  157 us (96%)
  local copies, waits for them, and re-layouts  5.21 us (3%)
    pallas_call x1, Pallas kernels, shards(): pl.pallas_call(kernel, out_shape=(jax.ShapeDtypeStruct((ROWS, COLS, 128),...  157 us
    unnamed x13, local copies, waits for them, and re-layouts  5.21 us

profile of v5, /device:TPU:1, one launch (start us, length us, event | category | flops | bytes accessed | tf_op | source)
XLA Modules:
  0.0 163.2 jit_solution(3730963578772521266)
XLA Ops:
  0.6 157.3 %triangle_backward.1 = (bf16[30,240,128]{2,1,0:T(8,128)(2,1)}, f32[128,4,128]{2,1,0:T(4,128)}, f32[4,128]{1,0:T(4,128)}, f32[1,128]{1,0:T(1,128)}, f32[1,128]{1,0:T(1,128)}) custom-call(bf16[30,240,128]{2,1,0:T(8,128)(2,1)} %pair_hbm.1, bf16[32,120,240]{2,1,0:T(8,128)(2,1)} %cot_ref.1, bf16[128,4,128]{2,1,0:T(4,128)(2,1)} %weight_ref.1, ...), custom_call_target="tpu_custom_call" | custom-call | tf_op jit(solution)/shard_map/triangle_backward/pallas_call | solution.py:476
  157.9 0.0 copy-start
  157.9 0.0 copy-start.1
  157.9 0.0 copy-start.3
  157.9 0.0 copy-start.2
  158.0 2.9 %copy.16 = bf16[30,240,128]{2,1,0:T(8,128)(2,1)} copy(bf16[30,240,128]{2,1,0:T(8,128)(2,1)} %get-tuple-element.20) | data formatting | bytes 3686400
  160.8 0.0 copy-done
  160.8 0.7 copy.17
  161.5 0.0 copy-done.1
  161.6 0.6 copy.18
  162.1 0.0 copy-done.3
  162.1 0.5 copy.19
  162.6 0.0 copy-done.2
  162.6 0.5 copy.20
Async XLA Ops:
  157.9 2.9 %copy-start = (f32[128,4,128]{2,1,0:T(4,128)S(1)}, f32[128,4,128]{2,1,0:T(4,128)}, u32[]{:S(2)}) copy-start(f32[128,4,128]{2,1,0:T(4,128)} %get-tuple-element.21) | copy-start | bytes 786436
  157.9 3.6 %copy-start.1 = (f32[4,128]{1,0:T(4,128)S(1)}, f32[4,128]{1,0:T(4,128)}, u32[]{:S(2)}) copy-start(f32[4,128]{1,0:T(4,128)} %get-tuple-element.22) | copy-start | bytes 6148
  157.9 4.2 %copy-start.3 = (f32[1,128]{1,0:T(1,128)S(1)}, f32[1,128]{1,0:T(1,128)}, u32[]{:S(2)}) copy-start(f32[1,128]{1,0:T(1,128)} %get-tuple-element.13) | copy-start | bytes 1540
  157.9 4.7 %copy-start.2 = (f32[1,128]{1,0:T(1,128)S(1)}, f32[1,128]{1,0:T(1,128)}, u32[]{:S(2)}) copy-start(f32[1,128]{1,0:T(1,128)} %get-tuple-element.14) | copy-start | bytes 1540
